TPU v7x, 32 devices: a whole 2x2x4 slice. The times are simulated.
32 devices in a mesh: section: 2 (over core), seq: 4 (over z), head: 4 (over y, x).
Axes of the slice: x: 2, y: 2, z: 4, core: 2. Of those that a mesh axis runs over, the one named last changes fastest.
Arguments:
- hidden_in: float32 [4, 2048, 768], P(None, 'seq'), may hold values from -6 to 6
- out_grad: float32 [4, 2048, 768], P(None, 'seq'), may hold values from -6 to 6
- norm_gain: float32 [2, 768], P('section'), may hold values from 0.5 to 1.5
- input_weight: bfloat16 [2, 768, 2, 1536], P('section', None, None, 'head'), may hold values from -0.21875 to 0.21875
- bc_weight: bfloat16 [2, 768, 256], P('section'), may hold values from -0.21875 to 0.21875
- step_size_weight: bfloat16 [2, 768, 24], P('section', None, 'head'), may hold values from -0.21875 to 0.21875
- conv_inner: float32 [2, 4, 1536], P('section', None, 'head'), may hold values from -3 to 3
- conv_shared: float32 [2, 4, 256], P('section'), may hold values from -3 to 3
- bias_inner: float32 [2, 1536], P('section', 'head'), may hold values from -1.5 to 1.5
- bias_shared: float32 [2, 256], P('section'), may hold values from -1.5 to 1.5
- step_bias: float32 [2, 24], P('section', 'head'), may hold values from -5 to -3
- decay_log: float32 [2, 24], P('section', 'head'), may hold values from -6.5 to 0.5
- skip_gain: float32 [2, 24], P('section', 'head'), may hold values from 0.5 to 1.5
- inner_gain: float32 [2, 1536], P('section', 'head'), may hold values from 0.5 to 1.5
- output_weight: bfloat16 [2, 1536, 768], P('section', 'head'), may hold values from -0.15625 to 0.15625
Outputs:
- hidden_out: float32 [2, 4, 2048, 768], P('section', None, 'seq')
- input_grad: float32 [2, 4, 2048, 768], P('section', None, 'seq')
- norm_gain_grad: float32 [2, 768], P('section')
- proj_weight_grad: float32 [2, 768, 2, 1536], P('section', None, None, 'head')
- shared_weight_grad: float32 [2, 768, 256], P('section')
- step_weight_grad: float32 [2, 768, 24], P('section', None, 'head')
- conv_inner_grad: float32 [2, 4, 1536], P('section', None, 'head')
- conv_shared_grad: float32 [2, 4, 256], P('section')
- bias_inner_grad: float32 [2, 1536], P('section', 'head')
- bias_shared_grad: float32 [2, 256], P('section')
- step_bias_grad: float32 [2, 24], P('section', 'head')
- decay_log_grad: float32 [2, 24], P('section', 'head')
- skip_gain_grad: float32 [2, 24], P('section', 'head')
- inner_gain_grad: float32 [2, 1536], P('section', 'head')
- down_weight_grad: float32 [2, 1536, 768], P('section', 'head')
All inputs are finite; a program needn't handle non-finite values.
Results may differ from a plain program's by a relative error of at most 0.014.
The roundings to bfloat16 on the way count: a program that leaves them out, or rounds other values in their place, can miss the bound.
Values sent between devices are 32-bit elements; how exact they have to be, the bound alone decides.
A program may use at most 256 MiB of HBM per device.

v0:
```python
import jax
import jax.numpy as jnp
from jax import lax
from jax.sharding import PartitionSpec as P

DI = 1536
P_SIZE = 64
N = 128
CONV = 4
SCAN_BLOCK = 256
MICRO = 2
SEQ_MB = 2


EPS = 1e-05
HIGHEST_PRECISION = lax.Precision.HIGHEST


def carried_in(part, axis, combine, identity, reverse):
    count = lax.axis_size(axis)
    place = lax.axis_index(axis)
    ahead = count - 1 - place if reverse else place
    gathered = jax.tree.map(lambda a: lax.all_gather(a, axis), part)
    state = jax.tree.map(lambda a, e: jnp.zeros_like(a) + jnp.asarray(e, a.dtype), part, identity)

    def one(lap, state):
        source = count - 1 - lap if reverse else lap
        return combine(
            state, jax.tree.map(lambda a: lax.dynamic_index_in_dim(a, source, 0, False), gathered)
        )

    return lax.fori_loop(0, ahead, one, state)


def passed_along(x, axis, by):
    length = lax.axis_size(axis)
    pairs = [(i, i + by) for i in range(length) if 0 <= i + by < length]
    return lax.ppermute(x, axis, pairs)


def norm_piece(hidden, gain):
    return hidden * lax.rsqrt(jnp.mean(hidden * hidden, axis=-1, keepdims=True) + EPS) * gain


def conv_silu(padded, kernel, shift):
    length = padded.shape[1] - kernel.shape[0] + 1
    total = shift
    for offset in range(kernel.shape[0]):
        total = total + kernel[offset] * padded[:, offset : offset + length]
    return jax.nn.silu(total)


def block_terms(inner_x, b_mat, c_mat, step_size, rate):
    cumulative = jnp.cumsum(step_size * rate, axis=1)
    steps = inner_x.shape[1]
    lower = jnp.arange(steps)[:, None] >= jnp.arange(steps)[None, :]
    spread = cumulative[:, :, None, :] - cumulative[:, None, :, :]
    decays = jnp.exp(jnp.where(lower[None, :, :, None], spread, -1e30))
    intersection = jnp.einsum("stn,sun->stu", c_mat, b_mat, precision=HIGHEST_PRECISION)
    mixing = intersection[..., None] * decays * step_size[:, None, :, :]
    y_intra = jnp.einsum("stuh,suhp->sthp", mixing, inner_x, precision=HIGHEST_PRECISION)
    tail = jnp.exp(cumulative[:, -1:, :] - cumulative) * step_size
    state = jnp.einsum("suh,suhp,sun->shpn", tail, inner_x, b_mat, precision=HIGHEST_PRECISION)
    return (y_intra, state, cumulative)


def carried(c_mat, cumulative, start):
    return jnp.exp(cumulative)[..., None] * jnp.einsum(
        "stn,shpn->sthp", c_mat, start, precision=HIGHEST_PRECISION
    )


def mixer_front(extended, step_logits, kernel, shift, step_bias, decay_log, skip_gain):
    group, padded_len, channels = extended.shape
    steps_dev = padded_len - CONV + 1
    heads_local = decay_log.shape[0]
    inner_local = heads_local * P_SIZE
    conv_out = conv_silu(extended, kernel, shift)
    inner_x = conv_out[..., :inner_local].reshape(group, steps_dev, heads_local, P_SIZE)
    b_mat = conv_out[..., inner_local : inner_local + N]
    c_mat = conv_out[..., inner_local + N :]
    step_size = jax.nn.softplus(step_logits + step_bias)
    rate = -jnp.exp(decay_log)
    block = min(SCAN_BLOCK, steps_dev)
    blocks = steps_dev // block

    def cut(values):
        return jnp.moveaxis(values.reshape((group, blocks, block) + values.shape[2:]), 1, 0)

    def block_step(start, pieces):
        x_block, b_block, c_block, s_block = pieces
        y_intra, state, block_cum = block_terms(x_block, b_block, c_block, s_block, rate)
        y_block = y_intra + carried(c_block, block_cum, start)
        new_start = jnp.exp(block_cum[:, -1])[..., None, None] * start + state
        return (new_start, y_block)

    start_zero = jnp.zeros((group, heads_local, P_SIZE, N), jnp.float32)
    final_state, y_blocks = lax.scan(
        jax.checkpoint(block_step),
        start_zero,
        (cut(inner_x), cut(b_mat), cut(c_mat), cut(step_size)),
    )
    y_local = jnp.moveaxis(y_blocks, 0, 1).reshape(group, steps_dev, heads_local, P_SIZE)
    cumulative = jnp.cumsum(step_size * rate, axis=1)
    return (
        y_local + skip_gain[:, None] * inner_x,
        final_state,
        cumulative[:, -1],
        cumulative,
        c_mat,
    )


def forward_combine(earlier, later):
    return (earlier[0] * later[0], later[0][..., None, None] * earlier[1] + later[1])


def backward_combine(earlier, later):
    return (earlier[0] * later[0], later[1] + later[0][..., None, None] * earlier[1])


def pass_states(state, log_decay):
    decay = jnp.exp(log_decay)
    _, start = carried_in(
        (decay, state), "seq", forward_combine, (jnp.ones_like(decay), jnp.zeros_like(state)), False
    )
    return (start, decay)


def pass_grads(start_grad, kept_decay):
    _, total = carried_in(
        (kept_decay, start_grad),
        "seq",
        backward_combine,
        (jnp.ones_like(kept_decay), jnp.zeros_like(start_grad)),
        True,
    )
    return total


def rows_product(left, right):
    return lax.dot_general(
        left, right, (((0,), (0,)), ((), ())), preferred_element_type=jnp.float32
    )


def layer_forward(current, weights):
    gain, w_main, w_shared, kernel, shift, step_bias, decay_log, skip_gain, inner_gain, w_down = (
        weights
    )
    group, steps_dev, width = current.shape
    inner_local = inner_gain.shape[0]
    heads_local = decay_log.shape[0]
    normalized_input, norm_vjp = jax.vjp(norm_piece, current, gain)
    flat_rows = normalized_input.astype(jnp.bfloat16).reshape(group * steps_dev, width)
    main_proj = jnp.dot(flat_rows, w_main, preferred_element_type=jnp.float32)
    shared_proj = jnp.dot(flat_rows, w_shared, preferred_element_type=jnp.float32)
    gate_logits = main_proj[:, :inner_local].reshape(group, steps_dev, inner_local)
    projected_mixer_input = main_proj[:, inner_local : 2 * inner_local]
    step_logits = main_proj[:, 2 * inner_local :].reshape(group, steps_dev, heads_local)
    mixed_in = jnp.concatenate([projected_mixer_input, shared_proj], axis=1).reshape(
        group, steps_dev, -1
    )
    rim_rows = mixed_in[:, steps_dev - (CONV - 1) :]
    before = passed_along(rim_rows, "seq", 1)
    extended = jnp.concatenate([before, mixed_in], axis=1)
    front, front_vjp = jax.vjp(
        mixer_front, extended, step_logits, kernel, shift, step_bias, decay_log, skip_gain
    )
    y_local, state, log_decay, cumulative, c_mat = front
    start, kept_decay = pass_states(state, log_decay)
    y_carry, carry_vjp = jax.vjp(carried, c_mat, cumulative, start)
    mixed_out = (y_local + y_carry).reshape(group, steps_dev, inner_local)
    gated = mixed_out * jax.nn.silu(gate_logits)
    total = lax.psum(jnp.sum(gated * gated, axis=-1), "head")
    rstd = lax.rsqrt(total / DI + EPS)[..., None]
    normalized_output = (
        (gated * rstd * inner_gain).astype(jnp.bfloat16).reshape(group * steps_dev, inner_local)
    )
    partial_value = jnp.dot(normalized_output, w_down, preferred_element_type=jnp.float32)
    branch_output = lax.psum(partial_value, "head")
    result = current + branch_output.reshape(group, steps_dev, width)
    kept = (
        flat_rows,
        norm_vjp,
        gate_logits,
        mixed_out,
        gated,
        rstd,
        normalized_output,
        front_vjp,
        carry_vjp,
        start,
        log_decay,
        kept_decay,
    )
    return (result, kept)


def layer_backward(cotangent, kept, weights):
    gain, w_main, w_shared, kernel, shift, step_bias, decay_log, skip_gain, inner_gain, w_down = (
        weights
    )
    (
        flat_rows,
        norm_vjp,
        gate_logits,
        mixed_out,
        gated,
        rstd,
        normalized_output,
        front_vjp,
        carry_vjp,
        start,
        log_decay,
        kept_decay,
    ) = kept
    group, steps_dev, width = cotangent.shape
    inner_local = inner_gain.shape[0]
    heads_local = decay_log.shape[0]
    down_grad = cotangent.astype(jnp.bfloat16).reshape(group * steps_dev, width)
    d_down = rows_product(normalized_output, down_grad)
    d_normed = lax.dot_general(
        down_grad, w_down, (((1,), (1,)), ((), ())), preferred_element_type=jnp.float32
    )
    d_normed = d_normed.reshape(group, steps_dev, inner_local)
    d_inner_gain = jnp.sum(d_normed * gated * rstd, axis=(0, 1))
    scaled_grad = d_normed * inner_gain
    dot_total = lax.psum(jnp.sum(scaled_grad * gated, axis=-1), "head")
    d_gated = rstd * scaled_grad - gated * rstd * rstd * rstd * dot_total[..., None] / DI
    sigmoid_gate = jax.nn.sigmoid(gate_logits)
    d_mixed = (d_gated * gate_logits * sigmoid_gate).reshape(group, steps_dev, heads_local, P_SIZE)
    d_gate = d_gated * mixed_out * sigmoid_gate * (1.0 + gate_logits * (1.0 - sigmoid_gate))
    d_cmat, d_cumulative, d_start = carry_vjp(d_mixed)
    state_grad = pass_grads(d_start, kept_decay)
    d_log = jnp.exp(log_decay) * jnp.sum(state_grad * start, axis=(2, 3))
    d_ext, d_dt, d_kernel, d_shift, d_bias_step, d_decay, d_skip = front_vjp(
        (d_mixed, state_grad, d_log, d_cumulative, d_cmat)
    )
    back_rows = passed_along(d_ext[:, : CONV - 1], "seq", -1)
    d_in_mix = d_ext[:, CONV - 1 :] + jnp.pad(
        back_rows, ((0, 0), (steps_dev - CONV + 1, 0), (0, 0))
    )
    rows = group * steps_dev
    d_main = jnp.concatenate(
        [
            d_gate.reshape(rows, inner_local),
            d_in_mix[..., :inner_local].reshape(rows, inner_local),
            d_dt.reshape(rows, heads_local),
        ],
        axis=1,
    ).astype(jnp.bfloat16)
    d_shared = d_in_mix[..., inner_local:].reshape(rows, 2 * N)
    d_main_w = rows_product(flat_rows, d_main)
    d_shared_w = lax.dot_general(
        flat_rows.astype(jnp.float32),
        d_shared,
        (((0,), (0,)), ((), ())),
        precision=HIGHEST_PRECISION,
    )
    d_normed_in = lax.dot_general(
        d_main, w_main, (((1,), (1,)), ((), ())), preferred_element_type=jnp.float32
    )
    d_normed_in = d_normed_in + lax.dot_general(
        d_shared,
        w_shared.astype(jnp.float32),
        (((1,), (1,)), ((), ())),
        precision=HIGHEST_PRECISION,
    )
    d_hidden, d_gain = norm_vjp(d_normed_in.reshape(group, steps_dev, width))
    input_total = cotangent + lax.psum(d_hidden, "head")
    grads = (
        d_gain,
        d_main_w,
        d_shared_w,
        d_kernel,
        d_shift,
        d_bias_step,
        d_decay,
        d_skip,
        d_inner_gain,
        d_down,
    )
    return (input_total, grads)


def shards(
    hidden_in,
    out_grad,
    norm_gain,
    input_weight,
    bc_weight,
    step_size_weight,
    conv_inner,
    conv_shared,
    bias_inner,
    bias_shared,
    step_bias,
    decay_log,
    skip_gain,
    inner_gain,
    output_weight,
):
    section_index = lax.axis_index("section")
    seqs_all, steps_dev, width = hidden_in.shape
    inner_local = inner_gain.shape[1]
    rounds = MICRO + 1
    w_main = jnp.concatenate(
        [input_weight[0].reshape(width, 2 * inner_local), step_size_weight[0]], axis=1
    )
    kernel = jnp.concatenate([conv_inner[0], conv_shared[0]], axis=1)
    shift = jnp.concatenate([bias_inner[0], bias_shared[0]])
    weights = (
        norm_gain[0],
        w_main,
        bc_weight[0],
        kernel,
        shift,
        step_bias[0],
        decay_log[0],
        skip_gain[0],
        inner_gain[0],
        output_weight[0],
    )
    hidden_buf = jnp.zeros(hidden_in.shape, jnp.float32)
    received = jnp.zeros((SEQ_MB, steps_dev, width), jnp.float32)
    saved = []
    for turn in range(rounds):
        index = turn - section_index
        valid = (index >= 0) & (index < MICRO)
        offset = jnp.clip(index, 0, MICRO - 1) * SEQ_MB
        fresh = lax.dynamic_slice_in_dim(hidden_in, offset, SEQ_MB, 0)
        current = jnp.where(section_index == 0, fresh, received)
        result, kept = layer_forward(current, weights)
        hidden_buf = jnp.where(
            valid, lax.dynamic_update_slice_in_dim(hidden_buf, result, offset, 0), hidden_buf
        )
        saved.append(kept)
        if turn + 1 < rounds:
            received = passed_along(result, "section", 1)
    grad_buf = jnp.zeros(hidden_in.shape, jnp.float32)
    returned = jnp.zeros((SEQ_MB, steps_dev, width), jnp.float32)
    totals = None
    for turn in range(rounds):
        index = MICRO - turn - section_index
        valid = (index >= 0) & (index < MICRO)
        offset = jnp.clip(index, 0, MICRO - 1) * SEQ_MB
        fresh = lax.dynamic_slice_in_dim(out_grad, offset, SEQ_MB, 0)
        cotangent = jnp.where(section_index == 1, fresh, returned)
        input_total, grads = layer_backward(cotangent, saved[MICRO - turn], weights)
        grad_buf = jnp.where(
            valid, lax.dynamic_update_slice_in_dim(grad_buf, input_total, offset, 0), grad_buf
        )
        masked = [jnp.where(valid, value, 0.0) for value in grads]
        if totals is None:
            totals = masked
        else:
            totals = [left + right for left, right in zip(totals, masked)]
        if turn + 1 < rounds:
            returned = passed_along(input_total, "section", -1)
    (
        d_gain,
        d_main_w,
        d_shared_w,
        d_kernel,
        d_shift,
        d_bias_step,
        d_decay,
        d_skip,
        d_inner_gain,
        d_down,
    ) = totals
    conv_width = conv_inner.shape[1]
    main_sum, kernel_inner, shift_inner, bias_step_sum, decay_sum, skip_sum, inner_sum, down_sum = (
        lax.psum(
            (
                d_main_w,
                d_kernel[:, :inner_local],
                d_shift[:inner_local],
                d_bias_step,
                d_decay,
                d_skip,
                d_inner_gain,
                d_down,
            ),
            "seq",
        )
    )
    gain_sum, shared_sum, kernel_shared, shift_shared = lax.psum(
        (d_gain, d_shared_w, d_kernel[:, inner_local:], d_shift[inner_local:]), ("seq", "head")
    )
    proj_grad = main_sum[:, : 2 * inner_local].reshape(width, 2, inner_local)
    step_grad = main_sum[:, 2 * inner_local :]
    return (
        hidden_buf[None],
        grad_buf[None],
        gain_sum[None],
        proj_grad[None],
        shared_sum[None],
        step_grad[None],
        kernel_inner[None],
        kernel_shared[None],
        shift_inner[None],
        shift_shared[None],
        bias_step_sum[None],
        decay_sum[None],
        skip_sum[None],
        inner_sum[None],
        down_sum[None],
    )


def solution(mesh):
    in_specs = (
        P(None, "seq", None),
        P(None, "seq", None),
        P("section", None),
        P("section", None, None, "head"),
        P("section", None, None),
        P("section", None, "head"),
        P("section", None, "head"),
        P("section", None, None),
        P("section", "head"),
        P("section", None),
        P("section", "head"),
        P("section", "head"),
        P("section", "head"),
        P("section", "head"),
        P("section", "head", None),
    )
    out_specs = (
        P("section", None, "seq", None),
        P("section", None, "seq", None),
        P("section", None),
        P("section", None, None, "head"),
        P("section", None, None),
        P("section", None, "head"),
        P("section", None, "head"),
        P("section", None, None),
        P("section", "head"),
        P("section", None),
        P("section", "head"),
        P("section", "head"),
        P("section", "head"),
        P("section", "head"),
        P("section", "head", None),
    )
    return jax.shard_map(shards, mesh=mesh, in_specs=in_specs, out_specs=out_specs, check_vma=False)
```

profile of v0, /device:TPU:0, one launch (start us, length us, event | category | flops | bytes accessed | tf_op | source)
XLA Modules:
  0.0 1976.4 jit_solution(5218533598917908732)
XLA Ops:
  50.4 32.3 %while.207 = (s32[]{:T(128)}, f32[2,6,64,128]{3,2,1,0:T(8,128)S(1)}, f32[2,2,256,6,64]{2,4,3,1,0:T(8,128)}, f32[2,2,6,64,128]{4,3,2,1,0:T(8,128)}, f32[2,2,256,6...) while((s32[]{:T(128)}, f32[2,6,64,128]{3,2,1,0:T(8,128)S(1)}, ...), condition=%wide.region_4.6_spmd.clone, body=%wide.region_1.5_spmd.clone.sunk | while | flops 1413915648 | bytes 10578125 | solution.py:98
  108.9 12.2 all-gather.16.cloned.1.call-done
  143.5 87.8 %all-reduce.57.cloned.1.call-done = f32[2,512,768]{2,1,0:T(8,128)} async-done(((f32[2,512,768]{2,1,0:T(8,128)}), f32[2,512,768]{2,1,0:T(8,128)}) %all-reduce.57.cloned.1.call-update) | async-done | bytes 3145744 | tf_op jit(solution)/shard_map/psum | solution.py:181
  287.4 34.1 %while.208 = (s32[]{:T(128)}, f32[2,6,64,128]{3,2,1,0:T(8,128)S(1)}, f32[2,2,256,6,64]{2,4,3,1,0:T(8,128)}, f32[2,2,6,64,128]{4,3,2,1,0:T(8,128)}, f32[2,2,256,6...) while((s32[]{:T(128)}, f32[2,6,64,128]{3,2,1,0:T(8,128)S(1)}, ...), condition=%wide.region_16.18_spmd.clone, body=%wide.region_13.17_spmd.clone.sunk | while | flops 1413915648 | bytes 10578125 | solution.py:98
  348.4 11.0 all-gather.18.cloned.1.call-done
  381.8 87.8 %all-reduce.59.cloned.1.call-done = f32[2,512,768]{2,1,0:T(8,128)} async-done(((f32[2,512,768]{2,1,0:T(8,128)}), f32[2,512,768]{2,1,0:T(8,128)}) %all-reduce.59.cloned.1.call-update) | async-done | bytes 3145744 | tf_op jit(solution)/shard_map/psum | solution.py:181
  523.6 30.9 %while.209 = (s32[]{:T(128)}, f32[2,6,64,128]{3,2,1,0:T(8,128)S(1)}, f32[2,2,256,6,64]{2,4,3,1,0:T(8,128)}, f32[2,2,6,64,128]{4,3,2,1,0:T(8,128)}, f32[2,2,256,6...) while((s32[]{:T(128)}, f32[2,6,64,128]{3,2,1,0:T(8,128)S(1)}, ...), condition=%wide.region_28.30_spmd.clone, body=%wide.region_25.29_spmd.clone.sunk | while | flops 1413915648 | bytes 15558889 | solution.py:98
  566.8 10.9 all-gather.4
  580.4 12.0 all-gather.20.cloned.1.call-done
  642.1 32.9 %all-gather.22.cloned.1.call-done = f32[8,6,64,128]{3,2,1,0:T(8,128)} async-done(((f32[2,6,64,128]{3,2,1,0:T(8,128)}), f32[8,6,64,128]{3,2,1,0:T(8,128)}) %all-gather.22.cloned.1.call-update) | async-done | bytes 1572880 | tf_op jit(solution)/shard_map/all_gather | solution.py:23
  683.0 120.0 %while.210 = (s32[]{:T(128)}, f32[6]{0:T(128)}, f32[2,6,64,128]{3,2,1,0:T(8,128)S(1)}, f32[2,2,256,6,64]{2,4,3,1,0:T(8,128)}, f32[2,2,256,128]{3,2,1,0:T(8,128)}...) while((s32[]{:T(128)}, f32[6]{0:T(128)}, ...), condition=%wide.region_53.55_spmd.clone, body=%wide.region_40.54_spmd.clone.sunk | while | flops 3338321920 | bytes 59959368 | solution.py:98
  708.3 15.8 reduce-window.290
  768.0 15.8 reduce-window.290
  828.8 15.3 reduce-window.240
  864.0 87.5 %all-reduce.61.cloned.1.call-done = f32[2,512,768]{2,1,0:T(8,128)} async-done(((f32[2,512,768]{2,1,0:T(8,128)}), f32[2,512,768]{2,1,0:T(8,128)}) %all-reduce.61.cloned.1.call-update) | async-done | bytes 3145744 | tf_op jit(solution)/shard_map/psum | solution.py:271
  999.0 32.2 %all-gather.24.cloned.1.call-done = f32[8,6,64,128]{3,2,1,0:T(8,128)} async-done(((f32[2,6,64,128]{3,2,1,0:T(8,128)}), f32[8,6,64,128]{3,2,1,0:T(8,128)}) %all-gather.24.cloned.1.call-update) | async-done | bytes 1572880 | tf_op jit(solution)/shard_map/all_gather | solution.py:23
  1041.0 120.0 %while.211 = (s32[]{:T(128)}, f32[6]{0:T(128)}, f32[2,6,64,128]{3,2,1,0:T(8,128)S(1)}, f32[2,2,256,6,64]{2,4,3,1,0:T(8,128)}, f32[2,2,256,128]{3,2,1,0:T(8,128)}...) while((s32[]{:T(128)}, f32[6]{0:T(128)}, ...), condition=%wide.region_77.79_spmd.clone, body=%wide.region_64.78_spmd.clone.sunk | while | flops 3338321920 | bytes 59959368 | solution.py:98
  1066.5 15.7 reduce-window.294
  1126.2 15.7 reduce-window.294
  1188.8 15.3 reduce-window.242
  1224.1 87.5 %all-reduce.63.cloned.1.call-done = f32[2,512,768]{2,1,0:T(8,128)} async-done(((f32[2,512,768]{2,1,0:T(8,128)}), f32[2,512,768]{2,1,0:T(8,128)}) %all-reduce.63.cloned.1.call-update) | async-done | bytes 3145744 | tf_op jit(solution)/shard_map/psum | solution.py:271
  1375.9 15.5 all-gather.26.cloned.1.call-done
  1397.8 15.1 reduce-window.244
  1417.5 119.7 %while.212 = (s32[]{:T(128)}, f32[6]{0:T(128)}, f32[2,6,64,128]{3,2,1,0:T(8,128)S(1)}, f32[2,2,256,6,64]{2,4,3,1,0:T(8,128)}, f32[2,2,256,128]{3,2,1,0:T(8,128)}...) while((s32[]{:T(128)}, f32[6]{0:T(128)}, ...), condition=%wide.region_101.103_spmd.clone, body=%wide.region_88.102_spmd.clone.sunk | while | flops 3338321920 | bytes 59959368 | solution.py:98
  1442.8 15.7 reduce-window.298
  1502.4 15.7 reduce-window.298
  1603.6 18.4 all-reduce.47
  1629.2 41.1 %all-reduce.45 = (f32[1,768]{1,0:T(1,128)}, f32[1,4,256]{2,1,0:T(4,128)}, f32[1,256]{1,0:T(1,128)}) all-reduce(f32[1,768]{1,0:T(1,128)S(1)} %broadcast_in_dim.528, f32[1,4,256]{2,1,0:T(4,128)S(1)} %slice_bitcast_fusion.2, f32[1,256]{1,0:T(1,128)S(1)} %bitcast.1519), channel_id=1, replica_groups=mesh['section'=2,'seq'=4,'head'=4] {'seq','head'}, use_global_device_ids=true, to_apply=%region_111.113 | all-reduce | flops 2048 | bytes 16384 | tf_op jit(solution)/shard_map/psum | solution.py:389
  1670.3 37.4 %all-reduce.69.cloned.1.call-done = (f32[768,774]{0,1:T(8,128)}, f32[1,384,768]{2,1,0:T(8,128)}) async-done(((f32[768,774]{0,1:T(8,128)}, f32[1,384,768]{2,1,0:T(8,128)}), (f32[768,774]{0,1:T(8,128)}, f32[1,384,768]{2,1,0:T(8,128)})) %all-reduce.69.cloned.1.call-update) | async-done | bytes 3557392 | tf_op jit(solution)/shard_map/psum | solution.py:375
  1713.9 135.6 %all-reduce.67.cloned.1.call-done = (f32[2,512,768]{2,1,0:T(8,128)}, f32[2,512,768]{2,1,0:T(8,128)}) async-done(((f32[2,512,768]{2,1,0:T(8,128)}, f32[2,512,768]{2,1,0:T(8,128)}), (f32[2,512,768]{2,1,0:T(8,128)}, f32[2,512,768]{2,1,0:T(8,128)})) %all-reduce.67.cloned.1.call-update) | async-done | bytes 6291472 | tf_op jit(solution)/shard_map/psum | solution.py:181
  1849.5 11.5 bitcast_dynamic-update-slice_fusion.6
  1861.0 105.5 %all-reduce.65.cloned.1.call-done = f32[1,768,256]{2,1,0:T(8,128)} async-done(((f32[1,768,256]{2,1,0:T(8,128)}), f32[1,768,256]{2,1,0:T(8,128)}) %all-reduce.65.cloned.1.call-update) | async-done | bytes 786448 | tf_op jit(solution)/shard_map/psum | solution.py:389
  (1675 shorter events, 1001.1 us)
Async XLA Ops:
  7.2 131.9 %copy-start = (bf16[1,384,768]{2,1,0:T(8,128)(2,1)S(1)}, bf16[1,384,768]{2,1,0:T(8,128)(2,1)}, u32[]{:S(2)}) copy-start(bf16[1,384,768]{2,1,0:T(8,128)(2,1)} %param.54) | copy-start | bytes 1769476
  7.2 113.9 %all-gather.16.cloned.1.call-start = ((), (), s32[]{:S(2)}) async-start(), calls=%async_computation.5 | async-start | bytes 1966080 | tf_op jit(solution)/shard_map/all_gather | solution.py:23
  10.7 475.7 %copy-start.189 = (f32[768]{0:T(1024)}, f32[768]{0:T(1024)S(1)}, u32[]{:S(2)}) copy-start(f32[768]{0:T(1024)S(1)} %reduce.15) | copy-start | bytes 9220
  22.5 8.7 collective-permute-start
  31.2 472.9 %copy-start.213 = (f32[640]{0:T(1024)}, f32[640]{0:T(1024)S(1)}, u32[]{:S(2)}) copy-start(f32[640]{0:T(1024)S(1)} %get-tuple-element.2322) | copy-start | bytes 7684
  31.2 472.9 %copy-start.217 = (f32[640]{0:T(1024)}, f32[640]{0:T(1024)S(1)}, u32[]{:S(2)}) copy-start(f32[640]{0:T(1024)S(1)} %get-tuple-element.2323) | copy-start | bytes 7684
  83.5 147.8 %all-reduce.57.cloned.1.call-start = ((), (), s32[]{:S(2)}) async-start(), calls=%async_computation | async-start | bytes 6291456 | tf_op jit(solution)/shard_map/psum | solution.py:181
  92.1 32.0 %copy-start.184 = (f32[2,512,6]{1,2,0:T(8,128)}, f32[2,512,6]{1,2,0:T(8,128)S(1)}, u32[]{:S(2)}) copy-start(f32[2,512,6]{1,2,0:T(8,128)S(1)} %copy.1124) | copy-start | bytes 73732
  95.6 43.5 %copy-start.270 = (f32[384]{0:T(512)}, f32[384]{0:T(512)S(1)}, u32[]{:S(2)}) copy-start(f32[384]{0:T(512)S(1)} %reduce.21) | copy-start | bytes 4612
  143.4 215.9 %all-gather.18.cloned.1.call-start = ((), (), s32[]{:S(2)}) async-start(), calls=%async_computation.6 | async-start | bytes 1966080 | tf_op jit(solution)/shard_map/all_gather | solution.py:23
  239.9 7.3 collective-permute-start.1
  261.5 6.7 collective-permute-start.2
  322.3 147.3 %all-reduce.59.cloned.1.call-start = ((), (), s32[]{:S(2)}) async-start(), calls=%async_computation.1 | async-start | bytes 6291456 | tf_op jit(solution)/shard_map/psum | solution.py:181
  381.7 210.7 %all-gather.20.cloned.1.call-start = ((), (), s32[]{:S(2)}) async-start(), calls=%async_computation.7 | async-start | bytes 1966080 | tf_op jit(solution)/shard_map/all_gather | solution.py:23
  476.8 7.3 collective-permute-start.3
  498.2 5.9 collective-permute-start.4
  555.3 119.8 %all-gather.22.cloned.1.call-start = ((), (), s32[]{:S(2)}) async-start(), calls=%async_computation.8 | async-start | bytes 1966080 | tf_op jit(solution)/shard_map/all_gather | solution.py:23
  566.7 65.8 %copy-start.188 = (f32[2,512,6]{1,2,0:T(8,128)}, f32[2,512,6]{1,2,0:T(8,128)S(1)}, u32[]{:S(2)}) copy-start(f32[2,512,6]{1,2,0:T(8,128)S(1)} %copy.1162) | copy-start | bytes 73732
  592.9 85.8 %copy-start.36 = (f32[2,6,64,128]{3,2,1,0:T(8,128)}, f32[2,6,64,128]{3,2,1,0:T(8,128)S(1)}, u32[]{:S(2)}) copy-start(f32[2,6,64,128]{3,2,1,0:T(8,128)S(1)} %get-tuple-element.1541) | copy-start | bytes 1179652
  636.4 315.2 %all-reduce.61.cloned.1.call-start = ((), (), s32[]{:S(2)}) async-start(), calls=%async_computation.2 | async-start | bytes 6291456 | tf_op jit(solution)/shard_map/psum | solution.py:271
  825.0 26.7 %collective-permute-start.5 = (f32[2,3,640]{2,1,0:T(4,128)S(1)}, f32[2,3,640]{2,1,0:T(4,128)S(1)}, u32[]{:S(2)}, u32[]{:S(2)}) collective-permute-start(f32[2,3,640]{2,1,0:T(4,128)S(1)} %pad_add_fusion.8), channel_id=1, source_target_pairs={{4,0},{8,4},{12,8},{5,1},{9,5},{13,9},{6,2},{10,6},{14,10},{7,3},{... | collective-permute-start | bytes 46088 | tf_op jit(solution)/shard_map/ppermute | solution.py:38
  864.0 167.1 %all-gather.24.cloned.1.call-start = ((), (), s32[]{:S(2)}) async-start(), calls=%async_computation.9 | async-start | bytes 1966080 | tf_op jit(solution)/shard_map/all_gather | solution.py:23
  959.9 8.0 collective-permute-start.6
  993.9 317.8 %all-reduce.63.cloned.1.call-start = ((), (), s32[]{:S(2)}) async-start(), calls=%async_computation.3 | async-start | bytes 6291456 | tf_op jit(solution)/shard_map/psum | solution.py:271
  1185.1 26.9 %collective-permute-start.7 = (f32[2,3,640]{2,1,0:T(4,128)S(1)}, f32[2,3,640]{2,1,0:T(4,128)S(1)}, u32[]{:S(2)}, u32[]{:S(2)}) collective-permute-start(f32[2,3,640]{2,1,0:T(4,128)S(1)} %pad_add_fusion.7), channel_id=1, source_target_pairs={{4,0},{8,4},{12,8},{5,1},{9,5},{13,9},{6,2},{10,6},{14,10},{7,3},{... | collective-permute-start | bytes 46088 | tf_op jit(solution)/shard_map/ppermute | solution.py:38
  1224.1 167.3 %all-gather.26.cloned.1.call-start = ((), (), s32[]{:S(2)}) async-start(), calls=%async_computation.10 | async-start | bytes 1966080 | tf_op jit(solution)/shard_map/all_gather | solution.py:23
  1319.8 8.0 collective-permute-start.8
  1354.2 353.5 %all-reduce.69.cloned.1.call-start = ((), (), s32[]{:S(2)}) async-start(), calls=%async_computation.12 | async-start | bytes 7127040 | tf_op jit(solution)/shard_map/psum | solution.py:375
  1559.1 5.8 collective-permute-start.9
  1573.0 276.5 %all-reduce.67.cloned.1.call-start = ((), (), s32[]{:S(2)}) async-start(), calls=%async_computation.11 | async-start | bytes 12582912 | tf_op jit(solution)/shard_map/psum | solution.py:181
  1586.5 380.0 %all-reduce.65.cloned.1.call-start = ((), (), s32[]{:S(2)}) async-start(), calls=%async_computation.4 | async-start | bytes 1572864 | tf_op jit(solution)/shard_map/psum | solution.py:389
  1849.5 119.1 %copy-start.165 = (f32[1,384,768]{2,1,0:T(8,128)S(1)}, f32[1,384,768]{2,1,0:T(8,128)}, u32[]{:S(2)}) copy-start(f32[1,384,768]{2,1,0:T(8,128)} %get-tuple-element.3932) | copy-start | bytes 3538948
  (402 other events, 2194.2 us)
Sparse Core Ops, SparseCore 0:
  83.6 37.3 all-gather.15
  143.6 87.7 all-reduce.56
  322.4 36.9 all-gather.17
  381.8 87.7 all-reduce.58
  555.4 36.9 all-gather.19
  636.5 38.5 all-gather.21
  864.1 87.4 all-reduce.60
  994.0 37.0 all-gather.23
  1224.2 87.4 all-reduce.62
  1354.3 37.0 all-gather.25
  1573.1 134.4 all-reduce.68
  1711.4 138.0 all-reduce.66
  1856.2 110.3 all-reduce.64
where the time goes:
time: 1990 us; the launch traced here: 1980 us
  waiting for transfers between devices  759 us (38%)
  other arithmetic  431 us (22%)
  local copies, waits for them, and re-layouts  312 us (16%)
  matrix products  279 us (14%)
  blocking collectives  146 us (7%)
  starting transfers between devices  26.6 us (1%)
    psum x3, waiting for transfers between devices, layer_forward(): branch_output = lax.psum(partial_value, 'head')  311 us
    another operation x87, other arithmetic  225 us
    psum x2, waiting for transfers between devices, layer_backward(): input_total = cotangent + lax.psum(d_hidden, 'head')  175 us
    all_gather x6, waiting for transfers between devices, carried_in(): gathered = jax.tree.map(lambda a: lax.all_gather(a, axis), part)  116 us
    psum x1, waiting for transfers between devices, shards(): lax.psum((d_gain, d_shared_w, d_kernel[:, inner_local:], d_shift[inner_lo...  106 us
    dot_general x18, matrix products, block_terms(): jnp.einsum('stuh,suhp->sthp', mixing, inner_x, precision=HIGHEST_PRECISION)  80.9 us
    another operation x185, local copies, waits for them, and re-layouts  68.6 us
    dot_general x33, matrix products, carried(): jnp.einsum('stn,shpn->sthp', c_mat, start, precision=HIGHEST_PRECISION)  66.3 us
  transfers between devices with their start and end apart: 23, of which 18 were waited for; matrix products, arithmetic and copies ran while one was open for 10% of the time, Pallas kernels for 0%

commit v1 on v0

--- a/solution.py
+++ b/solution.py
@@ -8,34 +8,78 @@
 N = 128
 CONV = 4
 SCAN_BLOCK = 256
-MICRO = 2
-SEQ_MB = 2
 
 
 EPS = 1e-05
 HIGHEST_PRECISION = lax.Precision.HIGHEST
-
-
-def carried_in(part, axis, combine, identity, reverse):
-    count = lax.axis_size(axis)
-    place = lax.axis_index(axis)
-    ahead = count - 1 - place if reverse else place
-    gathered = jax.tree.map(lambda a: lax.all_gather(a, axis), part)
-    state = jax.tree.map(lambda a, e: jnp.zeros_like(a) + jnp.asarray(e, a.dtype), part, identity)
-
-    def one(lap, state):
-        source = count - 1 - lap if reverse else lap
-        return combine(
-            state, jax.tree.map(lambda a: lax.dynamic_index_in_dim(a, source, 0, False), gathered)
-        )
-
-    return lax.fori_loop(0, ahead, one, state)
+HIGH_PRECISION = lax.Precision.HIGH
+
+
+def running_sum(values):
+    steps = values.shape[1]
+    lower = (jnp.arange(steps)[:, None] >= jnp.arange(steps)[None, :]).astype(jnp.float32)
+    return jnp.einsum("ts,gsh->gth", lower, values, precision=HIGHEST_PRECISION)
+
+
+def between(log_decays, reverse):
+    count = lax.axis_size("seq")
+    place = lax.axis_index("seq")
+    sources = jnp.arange(count)
+    if reverse:
+        inside = (sources[None, :] > place) & (sources[None, :] < sources[:, None])
+        valid = sources > place
+    else:
+        inside = (sources[None, :] < place) & (sources[None, :] > sources[:, None])
+        valid = sources < place
+    log_sum = jnp.sum(
+        jnp.where(inside[:, :, None, None], log_decays[None], 0.0), axis=1
+    )
+    return jnp.where(valid[:, None, None], jnp.exp(log_sum), 0.0)
+
+
+def swapped(x):
+    return lax.ppermute(x, "section", [(0, 1), (1, 0)])
 
 
 def passed_along(x, axis, by):
     length = lax.axis_size(axis)
     pairs = [(i, i + by) for i in range(length) if 0 <= i + by < length]
     return lax.ppermute(x, axis, pairs)
+
+
+def traded(x, axis, bit):
+    count = lax.axis_size(axis)
+    return lax.ppermute(x, axis, [(i, i ^ bit) for i in range(count)])
+
+
+def head_sum(x):
+    count = lax.axis_size("head")
+    rows = x.shape[0]
+    if count != 4 or rows % 8:
+        return lax.psum(x, "head")
+    place = lax.axis_index("head")
+    parts = x.reshape(2, 4, rows // 8, x.shape[1])
+    sums = []
+    for part, bits in ((0, (1, 2)), (1, (2, 1))):
+        value = parts[part].reshape(2, 2, rows // 8, x.shape[1])
+        upper = [(place & bit) != 0 for bit in bits]
+        keep = jnp.where(upper[0], value[1], value[0])
+        give = jnp.where(upper[0], value[0], value[1])
+        value = keep + traded(give, "head", bits[0])
+        keep = jnp.where(upper[1], value[1], value[0])
+        give = jnp.where(upper[1], value[0], value[1])
+        sums.append([keep + traded(give, "head", bits[1]), upper, bits])
+    out = []
+    for value, upper, bits in sums:
+        came = traded(value, "head", bits[1])
+        value = jnp.where(
+            upper[1], jnp.concatenate([came, value]), jnp.concatenate([value, came])
+        )
+        came = traded(value, "head", bits[0])
+        out.append(
+            jnp.where(upper[0], jnp.concatenate([came, value]), jnp.concatenate([value, came]))
+        )
+    return jnp.concatenate(out)
 
 
 def norm_piece(hidden, gain):
@@ -51,22 +95,22 @@
 
 
 def block_terms(inner_x, b_mat, c_mat, step_size, rate):
-    cumulative = jnp.cumsum(step_size * rate, axis=1)
+    cumulative = running_sum(step_size * rate)
     steps = inner_x.shape[1]
     lower = jnp.arange(steps)[:, None] >= jnp.arange(steps)[None, :]
     spread = cumulative[:, :, None, :] - cumulative[:, None, :, :]
     decays = jnp.exp(jnp.where(lower[None, :, :, None], spread, -1e30))
-    intersection = jnp.einsum("stn,sun->stu", c_mat, b_mat, precision=HIGHEST_PRECISION)
+    intersection = jnp.einsum("stn,sun->stu", c_mat, b_mat, precision=HIGH_PRECISION)
     mixing = intersection[..., None] * decays * step_size[:, None, :, :]
-    y_intra = jnp.einsum("stuh,suhp->sthp", mixing, inner_x, precision=HIGHEST_PRECISION)
+    y_intra = jnp.einsum("stuh,suhp->sthp", mixing, inner_x, precision=HIGH_PRECISION)
     tail = jnp.exp(cumulative[:, -1:, :] - cumulative) * step_size
-    state = jnp.einsum("suh,suhp,sun->shpn", tail, inner_x, b_mat, precision=HIGHEST_PRECISION)
+    state = jnp.einsum("suh,suhp,sun->shpn", tail, inner_x, b_mat, precision=HIGH_PRECISION)
     return (y_intra, state, cumulative)
 
 
 def carried(c_mat, cumulative, start):
     return jnp.exp(cumulative)[..., None] * jnp.einsum(
-        "stn,shpn->sthp", c_mat, start, precision=HIGHEST_PRECISION
+        "stn,shpn->sthp", c_mat, start, precision=HIGH_PRECISION
     )
 
 
@@ -101,7 +145,7 @@
         (cut(inner_x), cut(b_mat), cut(c_mat), cut(step_size)),
     )
     y_local = jnp.moveaxis(y_blocks, 0, 1).reshape(group, steps_dev, heads_local, P_SIZE)
-    cumulative = jnp.cumsum(step_size * rate, axis=1)
+    cumulative = running_sum(step_size * rate)
     return (
         y_local + skip_gain[:, None] * inner_x,
         final_state,
@@ -111,31 +155,19 @@
     )
 
 
-def forward_combine(earlier, later):
-    return (earlier[0] * later[0], later[0][..., None, None] * earlier[1] + later[1])
-
-
-def backward_combine(earlier, later):
-    return (earlier[0] * later[0], later[1] + later[0][..., None, None] * earlier[1])
-
-
 def pass_states(state, log_decay):
-    decay = jnp.exp(log_decay)
-    _, start = carried_in(
-        (decay, state), "seq", forward_combine, (jnp.ones_like(decay), jnp.zeros_like(state)), False
-    )
-    return (start, decay)
-
-
-def pass_grads(start_grad, kept_decay):
-    _, total = carried_in(
-        (kept_decay, start_grad),
-        "seq",
-        backward_combine,
-        (jnp.ones_like(kept_decay), jnp.zeros_like(start_grad)),
-        True,
-    )
-    return total
+    group, heads, size, width = state.shape
+    row = jnp.broadcast_to(log_decay[:, :, None, None], (group, heads, 1, width))
+    gathered = lax.all_gather(jnp.concatenate([state, row], axis=2), "seq")
+    log_decays = gathered[:, :, :, size, 0]
+    weight = between(log_decays, False)
+    return (jnp.sum(weight[..., None, None] * gathered[:, :, :, :size], axis=0), log_decays)
+
+
+def pass_grads(start_grad, log_decays):
+    grads = lax.all_gather(start_grad, "seq")
+    weight = between(log_decays, True)
+    return jnp.sum(weight[..., None, None] * grads, axis=0)
 
 
 def rows_product(left, right):
@@ -178,7 +210,7 @@
         (gated * rstd * inner_gain).astype(jnp.bfloat16).reshape(group * steps_dev, inner_local)
     )
     partial_value = jnp.dot(normalized_output, w_down, preferred_element_type=jnp.float32)
-    branch_output = lax.psum(partial_value, "head")
+    branch_output = head_sum(partial_value)
     result = current + branch_output.reshape(group, steps_dev, width)
     kept = (
         flat_rows,
@@ -197,7 +229,7 @@
     return (result, kept)
 
 
-def layer_backward(cotangent, kept, weights):
+def layer_backward(cotangent, kept, weights, pending):
     gain, w_main, w_shared, kernel, shift, step_bias, decay_log, skip_gain, inner_gain, w_down = (
         weights
     )
@@ -232,7 +264,7 @@
     d_mixed = (d_gated * gate_logits * sigmoid_gate).reshape(group, steps_dev, heads_local, P_SIZE)
     d_gate = d_gated * mixed_out * sigmoid_gate * (1.0 + gate_logits * (1.0 - sigmoid_gate))
     d_cmat, d_cumulative, d_start = carry_vjp(d_mixed)
-    state_grad = pass_grads(d_start, kept_decay)
+    state_grad, pending = lax.optimization_barrier((pass_grads(d_start, kept_decay), pending))
     d_log = jnp.exp(log_decay) * jnp.sum(state_grad * start, axis=(2, 3))
     d_ext, d_dt, d_kernel, d_shift, d_bias_step, d_decay, d_skip = front_vjp(
         (d_mixed, state_grad, d_log, d_cumulative, d_cmat)
@@ -253,22 +285,24 @@
     d_shared = d_in_mix[..., inner_local:].reshape(rows, 2 * N)
     d_main_w = rows_product(flat_rows, d_main)
     d_shared_w = lax.dot_general(
-        flat_rows.astype(jnp.float32),
-        d_shared,
+        flat_rows,
+        d_shared.astype(jnp.bfloat16),
         (((0,), (0,)), ((), ())),
-        precision=HIGHEST_PRECISION,
+        preferred_element_type=jnp.float32,
     )
     d_normed_in = lax.dot_general(
         d_main, w_main, (((1,), (1,)), ((), ())), preferred_element_type=jnp.float32
     )
     d_normed_in = d_normed_in + lax.dot_general(
-        d_shared,
-        w_shared.astype(jnp.float32),
+        d_shared.astype(jnp.bfloat16),
+        w_shared,
         (((1,), (1,)), ((), ())),
-        precision=HIGHEST_PRECISION,
+        preferred_element_type=jnp.float32,
     )
     d_hidden, d_gain = norm_vjp(d_normed_in.reshape(group, steps_dev, width))
-    input_total = cotangent + lax.psum(d_hidden, "head")
+    input_total = cotangent + head_sum(d_hidden.reshape(group * steps_dev, width)).reshape(
+        group, steps_dev, width
+    )
     grads = (
         d_gain,
         d_main_w,
@@ -281,7 +315,30 @@
         d_inner_gain,
         d_down,
     )
-    return (input_total, grads)
+    return (input_total, grads, pending)
+
+
+def joined(values):
+    return jnp.concatenate([value.reshape(-1) for value in values])
+
+
+def stacked(flat, width):
+    rows = -(-flat.shape[0] // (8 * width)) * 8
+    return jnp.pad(flat, (0, rows * width - flat.shape[0])).reshape(rows, width)
+
+
+def total_terms(terms):
+    main_half, down_wide, shared_wide = terms
+    return lax.psum((main_half, down_wide, lax.psum(shared_wide, "head")), "seq")
+
+
+def parted(flat, likes):
+    out = []
+    at = 0
+    for like in likes:
+        out.append(flat[at : at + like.size].reshape(like.shape))
+        at += like.size
+    return out
 
 
 def shards(
@@ -301,16 +358,17 @@
     inner_gain,
     output_weight,
 ):
-    section_index = lax.axis_index("section")
+    section = lax.axis_index("section")
+    first = section == 0
     seqs_all, steps_dev, width = hidden_in.shape
     inner_local = inner_gain.shape[1]
-    rounds = MICRO + 1
+    mine = seqs_all // 2
     w_main = jnp.concatenate(
         [input_weight[0].reshape(width, 2 * inner_local), step_size_weight[0]], axis=1
     )
     kernel = jnp.concatenate([conv_inner[0], conv_shared[0]], axis=1)
     shift = jnp.concatenate([bias_inner[0], bias_shared[0]])
-    weights = (
+    own = (
         norm_gain[0],
         w_main,
         bc_weight[0],
@@ -322,78 +380,89 @@
         inner_gain[0],
         output_weight[0],
     )
-    hidden_buf = jnp.zeros(hidden_in.shape, jnp.float32)
-    received = jnp.zeros((SEQ_MB, steps_dev, width), jnp.float32)
+    here = first.astype(jnp.float32)
+    layers = ([], [])
+    for value in own:
+        mine32 = value.astype(jnp.float32)
+        other = swapped(mine32)
+        layers[0].append((mine32 * here + other * (1.0 - here)).astype(value.dtype))
+        layers[1].append((other * here + mine32 * (1.0 - here)).astype(value.dtype))
+    current = lax.dynamic_slice_in_dim(hidden_in, section * mine, mine, 0)
     saved = []
-    for turn in range(rounds):
-        index = turn - section_index
-        valid = (index >= 0) & (index < MICRO)
-        offset = jnp.clip(index, 0, MICRO - 1) * SEQ_MB
-        fresh = lax.dynamic_slice_in_dim(hidden_in, offset, SEQ_MB, 0)
-        current = jnp.where(section_index == 0, fresh, received)
-        result, kept = layer_forward(current, weights)
-        hidden_buf = jnp.where(
-            valid, lax.dynamic_update_slice_in_dim(hidden_buf, result, offset, 0), hidden_buf
+    hidden = []
+    for weights in layers:
+        current, kept = layer_forward(current, weights)
+        saved.append(kept)
+        hidden.append(current)
+    cotangent = lax.dynamic_slice_in_dim(out_grad, section * mine, mine, 0)
+
+    def whole(pair):
+        keep = jnp.where(first, pair[0], pair[1])
+        came = swapped(jnp.where(first, pair[1], pair[0]))
+        return jnp.where(
+            first, jnp.concatenate([keep, came]), jnp.concatenate([came, keep])
         )
-        saved.append(kept)
-        if turn + 1 < rounds:
-            received = passed_along(result, "section", 1)
-    grad_buf = jnp.zeros(hidden_in.shape, jnp.float32)
-    returned = jnp.zeros((SEQ_MB, steps_dev, width), jnp.float32)
-    totals = None
-    for turn in range(rounds):
-        index = MICRO - turn - section_index
-        valid = (index >= 0) & (index < MICRO)
-        offset = jnp.clip(index, 0, MICRO - 1) * SEQ_MB
-        fresh = lax.dynamic_slice_in_dim(out_grad, offset, SEQ_MB, 0)
-        cotangent = jnp.where(section_index == 1, fresh, returned)
-        input_total, grads = layer_backward(cotangent, saved[MICRO - turn], weights)
-        grad_buf = jnp.where(
-            valid, lax.dynamic_update_slice_in_dim(grad_buf, input_total, offset, 0), grad_buf
+
+    hidden_all = whole(hidden)
+    inputs = [None, None]
+    summed = [None, None]
+    pending = ()
+    for layer in (1, 0):
+        cotangent, grads, pending = layer_backward(
+            cotangent, saved[layer], layers[layer], pending
         )
-        masked = [jnp.where(valid, value, 0.0) for value in grads]
-        if totals is None:
-            totals = masked
-        else:
-            totals = [left + right for left, right in zip(totals, masked)]
-        if turn + 1 < rounds:
-            returned = passed_along(input_total, "section", -1)
-    (
-        d_gain,
-        d_main_w,
-        d_shared_w,
-        d_kernel,
-        d_shift,
-        d_bias_step,
-        d_decay,
-        d_skip,
-        d_inner_gain,
-        d_down,
-    ) = totals
-    conv_width = conv_inner.shape[1]
-    main_sum, kernel_inner, shift_inner, bias_step_sum, decay_sum, skip_sum, inner_sum, down_sum = (
-        lax.psum(
-            (
-                d_main_w,
-                d_kernel[:, :inner_local],
-                d_shift[:inner_local],
-                d_bias_step,
-                d_decay,
-                d_skip,
-                d_inner_gain,
-                d_down,
-            ),
-            "seq",
+        inputs[layer] = cotangent
+        d_gain, d_main, d_shared, d_kernel, d_shift, d_bias, d_decay, d_skip, d_inner, d_down = grads
+        if layer == 1:
+            cotangent, hidden_all = lax.optimization_barrier((cotangent, hidden_all))
+        halved = []
+        for value in (d_main, d_down, d_shared):
+            rows = value.shape[0] // 2
+            low, high = value[:rows], value[rows:]
+            halved.append(jnp.where(first, low, high) + swapped(jnp.where(first, high, low)))
+        small = joined([d_kernel[:, :inner_local], d_shift[:inner_local], d_bias, d_decay, d_skip, d_inner])
+        common = joined([d_gain, d_kernel[:, inner_local:], d_shift[inner_local:]])
+        common = common + swapped(common)
+        small = small + swapped(small)
+        shared_wide = jnp.concatenate([halved[2], stacked(common, halved[2].shape[1])])
+        down_wide = jnp.concatenate([halved[1], stacked(small, width)])
+        terms = (halved[0], down_wide, shared_wide)
+        if layer == 1:
+            pending = terms
+            continue
+        main_half, down_wide, shared_wide = lax.psum(pending, "seq")
+        summed[1] = (main_half, down_wide, lax.psum(shared_wide, "head"))
+        terms, summed[1] = lax.optimization_barrier((terms, summed[1]))
+        summed[0] = total_terms(terms)
+    shared_rows = halved[2].shape[0]
+    down_rows = halved[1].shape[0]
+    summed = [
+        (
+            main_half,
+            down_wide[:down_rows],
+            shared_wide[:shared_rows],
+            down_wide[down_rows:].reshape(-1),
+            shared_wide[shared_rows:].reshape(-1),
         )
-    )
-    gain_sum, shared_sum, kernel_shared, shift_shared = lax.psum(
-        (d_gain, d_shared_w, d_kernel[:, inner_local:], d_shift[inner_local:]), ("seq", "head")
+        for main_half, down_wide, shared_wide in summed
+    ]
+    grads_all = whole(inputs)
+    main_sum, down_sum, shared_sum = [
+        whole([summed[0][place], summed[1][place]]) for place in range(3)
+    ]
+    small, common = [jnp.where(first, summed[0][place], summed[1][place]) for place in (3, 4)]
+    kernel_inner, shift_inner, bias_step_sum, decay_sum, skip_sum, inner_sum = parted(
+        small,
+        [conv_inner[0], bias_inner[0], step_bias[0], decay_log[0], skip_gain[0], inner_gain[0]],
+    )
+    gain_sum, kernel_shared, shift_shared = parted(
+        common, [norm_gain[0], conv_shared[0], bias_shared[0]]
     )
     proj_grad = main_sum[:, : 2 * inner_local].reshape(width, 2, inner_local)
     step_grad = main_sum[:, 2 * inner_local :]
     return (
-        hidden_buf[None],
-        grad_buf[None],
+        hidden_all[None],
+        grads_all[None],
         gain_sum[None],
         proj_grad[None],
         shared_sum[None],

time: 1990 us -> 1010 us (0.51)
  waiting for transfers between devices: 759 us -> 413 us
  other arithmetic: 431 us -> 182 us
  local copies, waits for them, and re-layouts: 312 us -> 143 us
  matrix products: 279 us -> 141 us
  blocking collectives: 146 us -> 43.1 us
  starting transfers between devices: 26.6 us -> 54.7 us
    psum x7 -> x4, waiting for transfers between devices: 629 us -> 219 us  [the longest x1 89 us: total_terms(): lax.psum((main_half, down_wide, lax.psum(shared_wide, 'head')), 'seq')]
    another operation x87 -> x0, other arithmetic: 225 us -> none
    dot_general x99 -> x82, matrix products: 220 us -> 107 us  [the longest x12 40.4 us: block_terms(): jnp.einsum('stuh,suhp->sthp', mixing, inner_x, precision=HIGH_PRECISION)]
    ppermute x0 -> x57, waiting for transfers between devices: none -> 109 us  [the longest x32 106 us: traded(): return lax.ppermute(x, axis, [(i, i ^ bit) for i in range(count)])]
    psum x2 -> x0, blocking collectives: 59.5 us -> none  [the longest x1 41.1 us: shards(): lax.psum((d_gain, d_shared_w, d_kernel[:, inner_local:], d_shift[inner_lo...]
    another operation x185 -> x13, local copies, waits for them, and re-layouts: 68.6 us -> 12.5 us
    ppermute x0 -> x57, starting transfers between devices: none -> 44.1 us  [the longest x32 39.2 us: traded(): return lax.ppermute(x, axis, [(i, i ^ bit) for i in range(count)])]
    all_gather x6 -> x4, waiting for transfers between devices: 116 us -> 82.1 us  [the longest x2 62 us: pass_states(): gathered = lax.all_gather(jnp.concatenate([state, row], axis=2), 'seq')]
  transfers between devices with their start and end apart: 23 -> 69, of which waited for: 18 -> 30; matrix products, arithmetic and copies ran while one was open for 10% -> 26% of each run, Pallas kernels for 0% -> 0%
where the time goes in v1:
time: 1010 us; the launch traced here: 997 us
  waiting for transfers between devices  413 us (41%)
  other arithmetic  182 us (18%)
  local copies, waits for them, and re-layouts  143 us (14%)
  matrix products  141 us (14%)
  starting transfers between devices  54.7 us (5%)
  blocking collectives  43.1 us (4%)
  between operations  17.5 us (2%)
    ppermute x32, waiting for transfers between devices, traded(): return lax.ppermute(x, axis, [(i, i ^ bit) for i in range(count)])  106 us
    psum x1, waiting for transfers between devices, total_terms(): lax.psum((main_half, down_wide, lax.psum(shared_wide, 'head')), 'seq')  89 us
    all_gather x2, waiting for transfers between devices, pass_states(): gathered = lax.all_gather(jnp.concatenate([state, row], axis=2), 'seq')  62 us
    psum x1, waiting for transfers between devices, total_terms(): lax.psum(shared_wide, 'head')  47.6 us
    psum x1, waiting for transfers between devices, shards(): summed[1] = (main_half, down_wide, lax.psum(shared_wide, 'head'))  43 us
    dot_general x12, matrix products, block_terms(): jnp.einsum('stuh,suhp->sthp', mixing, inner_x, precision=HIGH_PRECISION)  40.4 us
    psum x1, waiting for transfers between devices, shards(): main_half, down_wide, shared_wide = lax.psum(pending, 'seq')  39.8 us
    ppermute x32, starting transfers between devices, traded(): return lax.ppermute(x, axis, [(i, i ^ bit) for i in range(count)])  39.2 us
  transfers between devices with their start and end apart: 69, of which 30 were waited for; matrix products, arithmetic and copies ran while one was open for 26% of the time, Pallas kernels for 0%

profile of v1, /device:TPU:0, one launch (start us, length us, event | category | flops | bytes accessed | tf_op | source)
XLA Modules:
  0.0 997.0 jit_solution(6668417724468279252)
XLA Ops:
  39.3 4.8 collective-permute-start.7
  56.3 14.1 %while.82 = (s32[]{:T(128)}, f32[2,6,64,128]{3,2,1,0:T(8,128)S(1)}, f32[2,2,256,6,64]{2,4,3,1,0:T(8,128)}, f32[2,2,6,64,128]{4,3,2,1,0:T(8,128)}, f32[2,2,256,6]...) while((s32[]{:T(128)}, f32[2,6,64,128]{3,2,1,0:T(8,128)S(1)}, ...), condition=%wide.region_2.4_spmd.clone, body=%wide.region_1.3_spmd.clone.sunk | while | flops 718447616 | bytes 20829652 | solution.py:142
  83.7 30.0 %all-gather.9.cloned.1.call-done = f32[8,6,65,128]{3,2,1,0:T(8,128)} async-done(((f32[2,6,65,128]{3,2,1,0:T(8,128)}), f32[8,6,65,128]{3,2,1,0:T(8,128)}) %all-gather.9.cloned.1.call-update) | async-done | bytes 1597456 | tf_op jit(solution)/shard_map/all_gather | solution.py:161
  120.6 10.0 %psum.84 = f32[2,512]{1,0:T(2,128)S(1)} all-reduce(f32[2,512]{1,0:T(2,128)S(1)} %get-tuple-element.1377), channel_id=1, replica_groups=mesh['section'=2,'seq'=4,'head'=4] {'head'}, use_global_device_ids=true, to_apply=%region_6.8 | all-reduce | flops 1024 | bytes 8192 | tf_op jit(solution)/shard_map/psum | solution.py:207
  137.6 16.2 %collective-permute-done.11 = f32[2,128,768]{2,1,0:T(8,128)S(1)} collective-permute-done((f32[2,128,768]{2,1,0:T(8,128)S(1)}, f32[2,128,768]{2,1,0:T(8,128)S(1)}, u32[]{:S(2)}, u32[]{:S(2)}) %collective-permute-start.11) | collective-permute-done | bytes 786464 | tf_op jit(solution)/shard_map/ppermute | solution.py:52
  157.2 6.0 collective-permute-done.12
  165.4 5.7 collective-permute-done.13
  177.3 11.4 %collective-permute-done.14 = f32[256,768]{1,0:T(8,128)S(1)} collective-permute-done((f32[256,768]{1,0:T(8,128)S(1)}, f32[256,768]{1,0:T(8,128)S(1)}, u32[]{:S(2)}, u32[]{:S(2)}) %collective-permute-start.14) | collective-permute-done | bytes 786464 | tf_op jit(solution)/shard_map/ppermute | solution.py:52
  220.5 15.3 %while.83 = (s32[]{:T(128)}, f32[2,6,64,128]{3,2,1,0:T(8,128)S(1)}, f32[2,2,256,6,64]{2,4,3,1,0:T(8,128)}, f32[2,2,6,64,128]{4,3,2,1,0:T(8,128)}, f32[2,2,256,6]...) while((s32[]{:T(128)}, f32[2,6,64,128]{3,2,1,0:T(8,128)S(1)}, ...), condition=%wide.region_9.11_spmd.clone, body=%wide.region_8.10_spmd.clone.sunk | while | flops 718447616 | bytes 20829652 | solution.py:142
  246.0 32.0 %all-gather.11.cloned.1.call-done = f32[8,6,65,128]{3,2,1,0:T(8,128)} async-done(((f32[2,6,65,128]{3,2,1,0:T(8,128)}), f32[8,6,65,128]{3,2,1,0:T(8,128)}) %all-gather.11.cloned.1.call-update) | async-done | bytes 1597456 | tf_op jit(solution)/shard_map/all_gather | solution.py:161
  286.0 10.0 %psum.85 = f32[2,512]{1,0:T(2,128)S(1)} all-reduce(f32[2,512]{1,0:T(2,128)S(1)} %get-tuple-element.1369), channel_id=1, replica_groups=mesh['section'=2,'seq'=4,'head'=4] {'head'}, use_global_device_ids=true, to_apply=%region_13.15 | all-reduce | flops 1024 | bytes 8192 | tf_op jit(solution)/shard_map/psum | solution.py:207
  307.6 5.3 multiply_reduce_fusion.25
  312.9 14.0 %psum.86 = f32[2,512]{1,0:T(2,128)S(1)} all-reduce(f32[2,512]{1,0:T(2,128)S(1)} %get-tuple-element.1236), channel_id=1, replica_groups=mesh['section'=2,'seq'=4,'head'=4] {'head'}, use_global_device_ids=true, to_apply=%region_15.17 | all-reduce | flops 1024 | bytes 8192 | tf_op jit(solution)/shard_map/psum | solution.py:261
  362.4 5.6 collective-permute-done.35
  380.9 53.2 %while.84 = (s32[]{:T(128)}, f32[6]{0:T(128)}, f32[2,6,64,128]{3,2,1,0:T(8,128)S(1)}, f32[2,2,256,6,64]{2,4,3,1,0:T(8,128)}, f32[2,2,256,128]{3,2,1,0:T(8,128)},...) while((s32[]{:T(128)}, f32[6]{0:T(128)}, ...), condition=%wide.region_27.29_spmd.clone, body=%wide.region_18.28_spmd.clone.sunk | while | flops 1695596544 | bytes 61484284 | solution.py:142
  387.7 5.0 fusion.529
  413.7 5.0 fusion.529
  479.4 10.8 %collective-permute-done.21 = f32[2,128,768]{2,1,0:T(8,128)} collective-permute-done((f32[2,128,768]{2,1,0:T(8,128)}, f32[2,128,768]{2,1,0:T(8,128)}, u32[]{:S(2)}, u32[]{:S(2)}) %collective-permute-start.21) | collective-permute-done | bytes 786464 | tf_op jit(solution)/shard_map/ppermute | solution.py:52
  521.7 10.2 %collective-permute-done.24 = f32[256,768]{1,0:T(8,128)S(1)} collective-permute-done((f32[256,768]{1,0:T(8,128)S(1)}, f32[256,768]{1,0:T(8,128)S(1)}, u32[]{:S(2)}, u32[]{:S(2)}) %collective-permute-start.24) | collective-permute-done | bytes 786464 | tf_op jit(solution)/shard_map/ppermute | solution.py:52
  535.0 5.3 maximum_select_fusion
  543.8 9.1 psum.87
  583.0 16.1 %all-gather.15.cloned.1.call-done = f32[8,6,64,128]{3,2,1,0:T(8,128)} async-done(((f32[2,6,64,128]{3,2,1,0:T(8,128)}), f32[8,6,64,128]{3,2,1,0:T(8,128)}) %all-gather.15.cloned.1.call-update) | async-done | bytes 1572880 | tf_op jit(solution)/shard_map/all_gather | solution.py:168
  605.1 47.5 %while.85 = (s32[]{:T(128)}, f32[6]{0:T(128)}, f32[2,6,64,128]{3,2,1,0:T(8,128)S(1)}, f32[2,2,256,6,64]{2,4,3,1,0:T(8,128)}, f32[2,2,256,128]{3,2,1,0:T(8,128)},...) while((s32[]{:T(128)}, f32[6]{0:T(128)}, ...), condition=%wide.region_55.57_spmd.clone, body=%wide.region_46.56_spmd.clone.sunk | while | flops 1695596544 | bytes 66772400 | solution.py:142
  611.6 5.0 fusion.557
  635.1 5.0 fusion.557
  694.3 13.1 %collective-permute-done.44 = f32[2,128,768]{2,1,0:T(8,128)S(1)} collective-permute-done((f32[2,128,768]{2,1,0:T(8,128)S(1)}, f32[2,128,768]{2,1,0:T(8,128)S(1)}, u32[]{:S(2)}, u32[]{:S(2)}) %collective-permute-start.44) | collective-permute-done | bytes 786464 | tf_op jit(solution)/shard_map/ppermute | solution.py:52
  713.6 5.1 collective-permute-done.45
  727.3 39.8 %all-reduce.45.cloned.1.call-done = (f32[384,774]{0,1:T(8,128)}, f32[200,768]{1,0:T(8,128)}, f32[392,256]{1,0:T(8,128)}) async-done(((f32[384,774]{0,1:T(8,128)}, f32[200,768]{1,0:T(8,128)}, f32[392,256]{1,0:T(8,128)}), (f32[384,774]{0,1:T(8,128)}, f32[200,768]{1,0:T(8,128)}, f32[392,256]{1,0:T(8,128)})) %all-reduce.45.cloned.1.call-update) | async-done | bytes 2204688 | tf_op jit(solution)/shard_map/psum | solution.py:433
  772.7 43.0 %all-reduce.39.cloned.1.call-done = f32[392,256]{1,0:T(8,128)} async-done(((f32[392,256]{1,0:T(8,128)}), f32[392,256]{1,0:T(8,128)}) %all-reduce.39.cloned.1.call-update) | async-done | bytes 401424 | tf_op jit(solution)/shard_map/psum | solution.py:434
  818.8 47.6 %all-reduce.41.cloned.1.call-done = f32[392,256]{1,0:T(8,128)} async-done(((f32[392,256]{1,0:T(8,128)}), f32[392,256]{1,0:T(8,128)}) %all-reduce.41.cloned.1.call-update) | async-done | bytes 401424 | tf_op jit(solution)/shard_map/psum | solution.py:332
  872.3 89.0 %all-reduce.43.cloned.1.call-done = (f32[392,256]{1,0:T(8,128)}, f32[384,774]{0,1:T(8,128)}, f32[200,768]{1,0:T(8,128)}) async-done(((f32[392,256]{1,0:T(8,128)}, f32[384,774]{0,1:T(8,128)}, f32[200,768]{1,0:T(8,128)}), (f32[392,256]{1,0:T(8,128)}, f32[384,774]{0,1:T(8,128)}, f32[200,768]{1,0:T(8,128)})) %all-reduce.43.cloned.1.call-update) | async-done | bytes 2204688 | tf_op jit(solution)/shard_map/psum | solution.py:332
  974.5 5.1 maximum_select_fusion.1
  (1183 shorter events, 511.9 us)
Async XLA Ops:
  7.2 106.5 %all-gather.9.cloned.1.call-start = ((), (), s32[]{:S(2)}) async-start(), calls=%async_computation.2 | async-start | bytes 2211840 | tf_op jit(solution)/shard_map/all_gather | solution.py:161
  71.3 206.7 %all-gather.11.cloned.1.call-start = ((), (), s32[]{:S(2)}) async-start(), calls=%async_computation.3 | async-start | bytes 2211840 | tf_op jit(solution)/shard_map/all_gather | solution.py:161
  136.5 17.3 %collective-permute-start.11 = (f32[2,128,768]{2,1,0:T(8,128)S(1)}, f32[2,128,768]{2,1,0:T(8,128)S(1)}, u32[]{:S(2)}, u32[]{:S(2)}) collective-permute-start(f32[2,128,768]{2,1,0:T(8,128)S(1)} %bitcast.909), channel_id=1, source_target_pairs={{0,1},{1,0},{2,3},{3,2},{4,5},{5,4},{6,7},{7,6},{8,9},{9,8},{10,11... | collective-permute-start | bytes 2359304 | tf_op jit(solution)/shard_map/ppermute | solution.py:52
  136.6 18.1 %collective-permute-start.15 = (f32[2,128,768]{2,1,0:T(8,128)S(1)}, f32[2,128,768]{2,1,0:T(8,128)S(1)}, u32[]{:S(2)}, u32[]{:S(2)}) collective-permute-start(f32[2,128,768]{2,1,0:T(8,128)S(1)} %bitcast.908), channel_id=1, source_target_pairs={{0,2},{1,3},{2,0},{3,1},{4,6},{5,7},{6,4},{7,5},{8,10},{9,11},{10,... | collective-permute-start | bytes 2359304 | tf_op jit(solution)/shard_map/ppermute | solution.py:52
  171.2 17.5 %collective-permute-start.14 = (f32[256,768]{1,0:T(8,128)S(1)}, f32[256,768]{1,0:T(8,128)S(1)}, u32[]{:S(2)}, u32[]{:S(2)}) collective-permute-start(f32[256,768]{1,0:T(8,128)S(1)} %maximum_select_fusion.12), channel_id=1, source_target_pairs={{0,1},{1,0},{2,3},{3,2},{4,5},{5,4},{6,7},{7,6},{8,9},{9,8},{10,11... | collective-permute-start | bytes 2359304 | tf_op jit(solution)/shard_map/ppermute | solution.py:52
  236.7 137.3 %all-gather.13.cloned.1.call-start = ((), (), s32[]{:S(2)}) async-start(), calls=%async_computation.4 | async-start | bytes 1966080 | tf_op jit(solution)/shard_map/all_gather | solution.py:168
  306.3 36.3 %collective-permute-start.29 = (f32[2,128,768]{2,1,0:T(8,128)}, f32[2,128,768]{2,1,0:T(8,128)}, u32[]{:S(2)}, u32[]{:S(2)}) collective-permute-start(f32[2,128,768]{2,1,0:T(8,128)} %bitcast.90), channel_id=1, source_target_pairs={{0,1},{1,0},{2,3},{3,2},{4,5},{5,4},{6,7},{7,6},{8,9},{9,8},{10,11... | collective-permute-start | bytes 2359304 | tf_op jit(solution)/shard_map/ppermute | solution.py:52
  306.3 39.1 %collective-permute-start.33 = (f32[2,128,768]{2,1,0:T(8,128)}, f32[2,128,768]{2,1,0:T(8,128)}, u32[]{:S(2)}, u32[]{:S(2)}) collective-permute-start(f32[2,128,768]{2,1,0:T(8,128)} %bitcast.94), channel_id=1, source_target_pairs={{0,2},{1,3},{2,0},{3,1},{4,6},{5,7},{6,4},{7,5},{8,10},{9,11},{10,... | collective-permute-start | bytes 2359304 | tf_op jit(solution)/shard_map/ppermute | solution.py:52
  338.6 260.5 %all-gather.15.cloned.1.call-start = ((), (), s32[]{:S(2)}) async-start(), calls=%async_computation.5 | async-start | bytes 1966080 | tf_op jit(solution)/shard_map/all_gather | solution.py:168
  348.9 129.1 %collective-permute-start.39 = (f32[192,768]{1,0:T(8,128)}, f32[192,768]{1,0:T(8,128)}, u32[]{:S(2)}, u32[]{:S(2)}) collective-permute-start(f32[192,768]{1,0:T(8,128)} %slice_select_fusion.20), channel_id=1, source_target_pairs={{0,16},{16,0},{1,17},{17,1},{2,18},{18,2},{3,19},{19,3},{4,20},{20... | collective-permute-start | bytes 1769480 | tf_op jit(solution)/shard_map/ppermute | solution.py:41
  361.6 93.7 %collective-permute-start.32 = (f32[256,768]{1,0:T(8,128)}, f32[256,768]{1,0:T(8,128)}, u32[]{:S(2)}, u32[]{:S(2)}) collective-permute-start(f32[256,768]{1,0:T(8,128)} %maximum_select_fusion.16), channel_id=1, source_target_pairs={{0,1},{1,0},{2,3},{3,2},{4,5},{5,4},{6,7},{7,6},{8,9},{9,8},{10,11... | collective-permute-start | bytes 2359304 | tf_op jit(solution)/shard_map/ppermute | solution.py:52
  368.9 88.5 %collective-permute-start.36 = (f32[256,768]{1,0:T(8,128)}, f32[256,768]{1,0:T(8,128)}, u32[]{:S(2)}, u32[]{:S(2)}) collective-permute-start(f32[256,768]{1,0:T(8,128)} %maximum_select_fusion.17), channel_id=1, source_target_pairs={{0,2},{1,3},{2,0},{3,1},{4,6},{5,7},{6,4},{7,5},{8,10},{9,11},{10,... | collective-permute-start | bytes 2359304 | tf_op jit(solution)/shard_map/ppermute | solution.py:52
  470.7 19.5 %collective-permute-start.21 = (f32[2,128,768]{2,1,0:T(8,128)}, f32[2,128,768]{2,1,0:T(8,128)}, u32[]{:S(2)}, u32[]{:S(2)}) collective-permute-start(f32[2,128,768]{2,1,0:T(8,128)} %bitcast.81), channel_id=1, source_target_pairs={{0,1},{1,0},{2,3},{3,2},{4,5},{5,4},{6,7},{7,6},{8,9},{9,8},{10,11... | collective-permute-start | bytes 2359304 | tf_op jit(solution)/shard_map/ppermute | solution.py:52
  476.5 20.7 %collective-permute-start.25 = (f32[2,128,768]{2,1,0:T(8,128)}, f32[2,128,768]{2,1,0:T(8,128)S(1)}, u32[]{:S(2)}, u32[]{:S(2)}) collective-permute-start(f32[2,128,768]{2,1,0:T(8,128)} %bitcast.85), channel_id=1, source_target_pairs={{0,2},{1,3},{2,0},{3,1},{4,6},{5,7},{6,4},{7,5},{8,10},{9,11},{10,... | collective-permute-start | bytes 2359304 | tf_op jit(solution)/shard_map/ppermute | solution.py:52
  479.3 53.8 %collective-permute-start.37 = (f32[2,512,768]{2,1,0:T(8,128)}, f32[2,512,768]{2,1,0:T(8,128)}, u32[]{:S(2)}, u32[]{:S(2)}) collective-permute-start(f32[2,512,768]{2,1,0:T(8,128)} %get-tuple-element.1414), channel_id=1, source_target_pairs={{0,16},{16,0},{1,17},{17,1},{2,18},{18,2},{3,19},{19,3},{4,20},{20... | collective-permute-start | bytes 9437192 | tf_op jit(solution)/shard_map/ppermute | solution.py:41
  513.9 18.0 %collective-permute-start.24 = (f32[256,768]{1,0:T(8,128)S(1)}, f32[256,768]{1,0:T(8,128)S(1)}, u32[]{:S(2)}, u32[]{:S(2)}) collective-permute-start(f32[256,768]{1,0:T(8,128)S(1)} %maximum_select_fusion.14), channel_id=1, source_target_pairs={{0,1},{1,0},{2,3},{3,2},{4,5},{5,4},{6,7},{7,6},{8,9},{9,8},{10,11... | collective-permute-start | bytes 2359304 | tf_op jit(solution)/shard_map/ppermute | solution.py:52
  515.9 16.1 %collective-permute-start.28 = (f32[256,768]{1,0:T(8,128)S(1)}, f32[256,768]{1,0:T(8,128)S(1)}, u32[]{:S(2)}, u32[]{:S(2)}) collective-permute-start(f32[256,768]{1,0:T(8,128)S(1)} %maximum_select_fusion.15), channel_id=1, source_target_pairs={{0,2},{1,3},{2,0},{3,1},{4,6},{5,7},{6,4},{7,5},{8,10},{9,11},{10,... | collective-permute-start | bytes 2359304 | tf_op jit(solution)/shard_map/ppermute | solution.py:52
  517.6 48.7 %collective-permute-start.41 = (f32[384,256]{1,0:T(8,128)}, f32[384,256]{1,0:T(8,128)S(1)}, u32[]{:S(2)}, u32[]{:S(2)}) collective-permute-start(f32[384,256]{1,0:T(8,128)} %slice_select_fusion.23), channel_id=1, source_target_pairs={{0,16},{16,0},{1,17},{17,1},{2,18},{18,2},{3,19},{19,3},{4,20},{20... | collective-permute-start | bytes 1179656 | tf_op jit(solution)/shard_map/ppermute | solution.py:41
  518.2 47.2 %collective-permute-start.42 = (f32[2048]{0:T(1024)}, f32[2048]{0:T(1024)}, u32[]{:S(2)}, u32[]{:S(2)}) collective-permute-start(f32[2048]{0:T(1024)} %pad_maximum_fusion.21), channel_id=1, source_target_pairs={{0,16},{16,0},{1,17},{17,1},{2,18},{18,2},{3,19},{19,3},{4,20},{20... | collective-permute-start | bytes 24584 | tf_op jit(solution)/shard_map/ppermute | solution.py:41
  562.4 204.7 %all-reduce.45.cloned.1.call-start = ((), (), s32[]{:S(2)}) async-start(), calls=%async_computation.7 | async-start | bytes 4415488 | tf_op jit(solution)/shard_map/psum | solution.py:433
  673.9 141.9 %all-reduce.39.cloned.1.call-start = ((), (), s32[]{:S(2)}) async-start(), calls=%async_computation | async-start | bytes 802816 | tf_op jit(solution)/shard_map/psum | solution.py:434
  681.1 40.9 %collective-permute-start.56 = (f32[384,256]{1,0:T(8,128)}, f32[384,256]{1,0:T(8,128)}, u32[]{:S(2)}, u32[]{:S(2)}) collective-permute-start(f32[384,256]{1,0:T(8,128)} %slice_select_fusion.22), channel_id=1, source_target_pairs={{0,16},{16,0},{1,17},{17,1},{2,18},{18,2},{3,19},{19,3},{4,20},{20... | collective-permute-start | bytes 1179656 | tf_op jit(solution)/shard_map/ppermute | solution.py:41
  688.1 19.3 %collective-permute-start.44 = (f32[2,128,768]{2,1,0:T(8,128)S(1)}, f32[2,128,768]{2,1,0:T(8,128)S(1)}, u32[]{:S(2)}, u32[]{:S(2)}) collective-permute-start(f32[2,128,768]{2,1,0:T(8,128)S(1)} %bitcast.907), channel_id=1, source_target_pairs={{0,1},{1,0},{2,3},{3,2},{4,5},{5,4},{6,7},{7,6},{8,9},{9,8},{10,11... | collective-permute-start | bytes 2359304 | tf_op jit(solution)/shard_map/ppermute | solution.py:52
  689.7 20.2 %collective-permute-start.48 = (f32[2,128,768]{2,1,0:T(8,128)}, f32[2,128,768]{2,1,0:T(8,128)}, u32[]{:S(2)}, u32[]{:S(2)}) collective-permute-start(f32[2,128,768]{2,1,0:T(8,128)} %bitcast.129), channel_id=1, source_target_pairs={{0,2},{1,3},{2,0},{3,1},{4,6},{5,7},{6,4},{7,5},{8,10},{9,11},{10,... | collective-permute-start | bytes 2359304 | tf_op jit(solution)/shard_map/ppermute | solution.py:52
  693.8 76.4 %collective-permute-start.53 = (f32[384,774]{0,1:T(8,128)}, f32[384,774]{0,1:T(8,128)}, u32[]{:S(2)}, u32[]{:S(2)}) collective-permute-start(f32[384,774]{0,1:T(8,128)} %slice_select_fusion), channel_id=1, source_target_pairs={{0,16},{16,0},{1,17},{17,1},{2,18},{18,2},{3,19},{19,3},{4,20},{20... | collective-permute-start | bytes 3566600 | tf_op jit(solution)/shard_map/ppermute | solution.py:41
  720.5 46.7 %collective-permute-start.46 = (f32[128,768]{1,0:T(8,128)}, f32[128,768]{1,0:T(8,128)}, u32[]{:S(2)}, u32[]{:S(2)}) collective-permute-start(f32[128,768]{1,0:T(8,128)} %bitcast_add_fusion.1), channel_id=1, source_target_pairs={{0,2},{1,3},{2,0},{3,1},{4,6},{5,7},{6,4},{7,5},{8,10},{9,11},{10,... | collective-permute-start | bytes 1179656 | tf_op jit(solution)/shard_map/ppermute | solution.py:52
  725.9 89.9 %collective-permute-start.50 = (f32[128,768]{1,0:T(8,128)}, f32[128,768]{1,0:T(8,128)}, u32[]{:S(2)}, u32[]{:S(2)}) collective-permute-start(f32[128,768]{1,0:T(8,128)} %bitcast_add_fusion), channel_id=1, source_target_pairs={{0,1},{1,0},{2,3},{3,2},{4,5},{5,4},{6,7},{7,6},{8,9},{9,8},{10,11... | collective-permute-start | bytes 1179656 | tf_op jit(solution)/shard_map/ppermute | solution.py:52
  767.1 99.3 %all-reduce.41.cloned.1.call-start = ((), (), s32[]{:S(2)}) async-start(), calls=%async_computation.1 | async-start | bytes 802816 | tf_op jit(solution)/shard_map/psum | solution.py:332
  768.7 97.7 %collective-permute-start.47 = (f32[256,768]{1,0:T(8,128)S(1)}, f32[256,768]{1,0:T(8,128)}, u32[]{:S(2)}, u32[]{:S(2)}) collective-permute-start(f32[256,768]{1,0:T(8,128)S(1)} %maximum_select_fusion.18), channel_id=1, source_target_pairs={{0,1},{1,0},{2,3},{3,2},{4,5},{5,4},{6,7},{7,6},{8,9},{9,8},{10,11... | collective-permute-start | bytes 2359304 | tf_op jit(solution)/shard_map/ppermute | solution.py:52
  815.8 145.6 %all-reduce.43.cloned.1.call-start = ((), (), s32[]{:S(2)}) async-start(), calls=%async_computation.6 | async-start | bytes 4415488 | tf_op jit(solution)/shard_map/psum | solution.py:332
  817.4 50.7 %collective-permute-start.51 = (f32[256,768]{1,0:T(8,128)S(1)}, f32[256,768]{1,0:T(8,128)S(1)}, u32[]{:S(2)}, u32[]{:S(2)}) collective-permute-start(f32[256,768]{1,0:T(8,128)S(1)} %maximum_select_fusion.19), channel_id=1, source_target_pairs={{0,2},{1,3},{2,0},{3,1},{4,6},{5,7},{6,4},{7,5},{8,10},{9,11},{10,... | collective-permute-start | bytes 2359304 | tf_op jit(solution)/shard_map/ppermute | solution.py:52
  872.3 102.1 %collective-permute-start.52 = (f32[2,512,768]{2,1,0:T(8,128)}, f32[2,512,768]{2,1,0:T(8,128)}, u32[]{:S(2)}, u32[]{:S(2)}) collective-permute-start(f32[2,512,768]{2,1,0:T(8,128)} %get-tuple-element.1412), channel_id=1, source_target_pairs={{0,16},{16,0},{1,17},{17,1},{2,18},{18,2},{3,19},{19,3},{4,20},{20... | collective-permute-start | bytes 9437192 | tf_op jit(solution)/shard_map/ppermute | solution.py:41
  (326 other events, 2257.1 us)
Sparse Core Ops, SparseCore 0:
  71.5 42.1 all-gather.8
  236.8 41.2 all-gather.10
  338.7 35.2 all-gather.12
  562.5 36.4 all-gather.14
  674.0 93.0 all-reduce.44
  770.0 45.7 all-reduce.38
  819.6 46.7 all-reduce.40
  869.6 91.7 all-reduce.42
